TPU v7x, 32 devices: a whole 2x2x4 slice. The times are simulated.
32 devices in a mesh: wide: 8 (over y, x, core), narrow: 4 (over z).
Axes of the slice: x: 2, y: 2, z: 4, core: 2. Of those that a mesh axis runs over, the one named last changes fastest.
Arguments:
- gcm_state: float32 [1024, 144], P('wide'), may hold values from -6 to 6
- crm_state: bfloat16 [2, 60, 256, 1024], P(None, None, 'narrow', 'wide'), may hold values from -6 to 6
- courant: float32 [60, 1024], P(None, 'wide'), may hold values from 0.1 to 0.6
- cloud_mask: int32 [60, 1024], P(None, 'wide'), may hold values 0 or 1
- level_down: float32 [60, 72], replicated, may hold values from -0.75 to 0.75
- level_up: float32 [72, 60], replicated, may hold values from -0.75 to 0.75
- column_map: int32 [1024], replicated, may hold values from 0 to 1023, as said below
Outputs:
- gcm_tendency: bfloat16 [1024, 144], P('wide')
- crm_new: bfloat16 [2, 60, 256, 1024], P(None, None, 'narrow', 'wide')
Inputs may be any that keep to these rules, and one draw needn't show every extreme that they name: column_map is a bijection onto 0 to 1023; the columns of one index of wide go to at most 32 slots of any one owner, and to exactly 32 slots of half of the owners.
All inputs are finite; a program needn't handle non-finite values. No bound on the sum of `cloud_mask` on one device may be relied on, other than what follows from the above.
Results may differ from a plain program's by a relative error of at most 0.0048.
Values may be sent and summed in bfloat16 or wider, within the bound.
A program may use at most 64 MiB of HBM per device.

v0:
```python
import jax
import jax.numpy as jnp
from jax import lax
from jax.sharding import PartitionSpec as P

CX = 256
SUB = 4


def with_halo(block, sides, width):
    for axis, dim in sides:
        count = lax.axis_size(axis)
        forward = [(i, i + 1) for i in range(count - 1)]
        forward.append((count - 1, 0))
        backward = [(target, source) for source, target in forward]
        low = lax.ppermute(
            lax.slice_in_dim(block, block.shape[dim] - width, None, axis=dim), axis, forward
        )
        high = lax.ppermute(lax.slice_in_dim(block, 0, width, axis=dim), axis, backward)
        block = jnp.concatenate([low, block, high], axis=dim)
    return block


def horizontal(padded, courant_now):
    left_cells = padded[:, :, :-2]
    middle = padded[:, :, 1:-1]
    right_cells = padded[:, :, 2:]
    return (
        middle
        + courant_now[None, :, None, :] * (left_cells - middle)
        + 0.15 * (right_cells - 2.0 * middle + left_cells)
    )


def column_physics(fields, forcing, cloudy):
    above_cells = jnp.concatenate([fields[:, 1:], fields[:, -1:]], axis=1)
    below_cells = jnp.concatenate([fields[:, :1], fields[:, :-1]], axis=1)
    fields = fields + 0.1 * (above_cells - 2.0 * fields + below_cells)
    fields = fields + 0.25 * forcing[:, :, None, :]
    moisture = fields[1]
    condensed = cloudy[:, None, :] * 0.3 * jnp.maximum(moisture, 0.0)
    return jnp.stack([fields[0] + 2.0 * condensed, moisture - condensed])


def shards(gcm_state, crm_state, courant, cloud_mask, level_down, level_up, column_map):
    wide_count = lax.axis_size("wide")
    wide_index = lax.axis_index("wide")
    columns = gcm_state.shape[0]
    capacity = 2 * columns // wide_count
    width_full = gcm_state.shape[1]
    levels = width_full // 2
    buffer_rows = wide_count * capacity
    my_targets = lax.dynamic_slice_in_dim(column_map, wide_index * columns, columns)
    my_owners = my_targets // columns
    position = jnp.arange(columns, dtype=jnp.int32)
    earlier = (my_owners[:, None] == my_owners[None, :]) & (position[None, :] < position[:, None])
    send_slot = my_owners * capacity + jnp.sum(earlier.astype(jnp.int32), axis=1)
    buffer_index = jnp.arange(buffer_rows, dtype=jnp.int32)
    send_match = (send_slot[None, :] == buffer_index[:, None]).astype(jnp.int32)
    send_filled = jnp.sum(send_match, axis=1) > 0
    send_source = jnp.sum(send_match * position[None, :], axis=1)
    all_targets = column_map.reshape(wide_count, columns)
    is_mine = all_targets // columns == wide_index
    rank_mine = jnp.cumsum(is_mine.astype(jnp.int32), axis=1) - 1
    local_slot = all_targets % columns
    within_cap = jnp.arange(capacity, dtype=jnp.int32)
    arrive_match = (
        is_mine[:, None, :] & (rank_mine[:, None, :] == within_cap[None, :, None])
    ).astype(jnp.int32)
    slot_of_buffer = jnp.sum(arrive_match * local_slot[:, None, :], axis=2).reshape(buffer_rows)
    arrive_filled = (jnp.sum(arrive_match, axis=2) > 0).reshape(buffer_rows)
    slot_match = (arrive_filled[:, None] & (slot_of_buffer[:, None] == position[None, :])).astype(
        jnp.int32
    )
    buffer_of_slot = jnp.sum(slot_match * buffer_index[:, None], axis=0)
    outgoing = gcm_state.astype(jnp.bfloat16)
    packed = jnp.where(send_filled[:, None], outgoing[send_source], jnp.zeros((), jnp.bfloat16))
    arrived = lax.all_to_all(packed, "wide", split_axis=0, concat_axis=0, tiled=True)
    slot_rows = arrived[buffer_of_slot].astype(jnp.float32).reshape(columns, 2, levels)
    forcing = jnp.einsum("sfm,lm->fls", slot_rows, level_down, precision=lax.Precision.HIGHEST)
    cloudy = cloud_mask.astype(jnp.float32)
    initial = crm_state.astype(jnp.float32)
    fields = with_halo(crm_state, (("narrow", 2),), SUB).astype(jnp.float32)
    for substep in range(SUB):
        fields = column_physics(horizontal(fields, courant), forcing, cloudy)
    crm_new = fields.astype(jnp.bfloat16)
    diff_sums = jnp.sum(fields - initial, axis=2)
    partial_term = jnp.einsum(
        "fls,ml->sfm", diff_sums, level_up, precision=lax.Precision.HIGHEST
    ) * (1.0 / (CX * SUB))
    partial_term = partial_term.reshape(columns, width_full)
    totals = lax.psum(partial_term, "narrow").astype(jnp.bfloat16)
    returned = lax.all_to_all(
        totals[slot_of_buffer], "wide", split_axis=0, concat_axis=0, tiled=True
    )
    gcm_tendency = returned[send_slot]
    return (gcm_tendency, crm_new)


def solution(mesh):
    placed = (
        P("wide", None),
        P(None, None, "narrow", "wide"),
        P(None, "wide"),
        P(None, "wide"),
        P(),
        P(),
        P(),
    )
    return jax.shard_map(
        shards,
        mesh=mesh,
        in_specs=placed,
        out_specs=(P("wide", None), P(None, None, "narrow", "wide")),
        check_vma=False,
    )
```

profile of v0, /device:TPU:0, one launch (start us, length us, event | category | flops | bytes accessed | tf_op | source)
XLA Modules:
  0.0 84.9 jit_solution(16330905190342435866)
XLA Ops:
  0.7 0.9 %and_select_fusion = s32[128]{0:T(128)S(1)} fusion(s32[1024]{0:T(1024)} %param.13, s32[]{:T(128)S(6)} %select_n.70), kind=kLoop, calls=%fused_computation.118 | loop fusion | flops 1920 | bytes 1028 | tf_op jit(solution)/shard_map/jit(floor_divide)/jit(_where)/select_n | solution.py:54
  1.6 0.2 convert_reduce_fusion.2
  1.7 0.8 compare_select_fusion.2
  2.5 0.2 convert_reduce_fusion.1
  2.7 0.9 %convert_element_type.39 = bf16[128,144]{0,1:T(8,128)(2,1)S(1)} convert(f32[128,144]{0,1:T(8,128)} %param.7) | non-fusion elementwise | flops 18432 | bytes 110592 | tf_op jit(solution)/shard_map/convert_element_type | solution.py:76
  3.6 0.1 copy.21
  3.8 1.2 %gather_fusion = bf16[256,144]{1,0:T(8,128)(2,1)S(1)} fusion(bf16[128,144]{1,0:T(8,128)(2,1)S(1)} %copy.21, s32[1024]{0:T(1024)S(1)} %pad_clamp_fusion.3), kind=kCustom, calls=%fused_computation | custom fusion | bytes 148480 | tf_op jit(solution)/shard_map/gather | solution.py:77
  5.0 0.8 broadcast_select_fusion
  5.7 5.2 %all-to-all-start = ((bf16[8,32,144]{2,1,0:T(8,128)(2,1)}), bf16[8,32,144]{2,1,0:T(8,128)(2,1)S(1)}, u32[]{:S(2)}, u32[]{:S(2)}) async-start(bf16[8,32,144]{2,1,0:T(8,128)(2,1)} %broadcast_select_fusion), calls=%async_computation | async-start | bytes 262144 | tf_op jit(solution)/shard_map/all_to_all | solution.py:78
  10.9 1.2 %fusion.63 = (bf16[2,60,4,128]{3,2,1,0:T(4,128)(2,1)S(1)}, bf16[2,60,4,128]{3,2,1,0:T(4,128)(2,1)S(1)}) fusion(bf16[2,60,64,128]{3,2,1,0:T(8,128)(2,1)} %param.8), kind=kLoop, calls=%fused_computation.134 | loop fusion | bytes 491520 | tf_op jit(solution)/shard_map/slice | solution.py:17
  12.1 1.6 %collective-permute-start = (bf16[2,60,4,128]{3,2,1,0:T(4,128)(2,1)S(1)}, bf16[2,60,4,128]{3,2,1,0:T(4,128)(2,1)S(1)}, u32[]{:S(2)}, u32[]{:S(2)}) collective-permute-start(bf16[2,60,4,128]{3,2,1,0:T(4,128)(2,1)S(1)} %get-tuple-element.42), channel_id=1, source_target_pairs={{0,1},{1,2},{2,3},{3,0},{4,5},{5,6},{6,7},{7,4},{8,9},{9,10},{10,1... | collective-permute-start | bytes 368648 | tf_op jit(solution)/shard_map/ppermute | solution.py:16
  13.7 2.2 %collective-permute-start.1 = (bf16[2,60,4,128]{3,2,1,0:T(4,128)(2,1)S(1)}, bf16[2,60,4,128]{3,2,1,0:T(4,128)(2,1)S(1)}, u32[]{:S(2)}, u32[]{:S(2)}) collective-permute-start(bf16[2,60,4,128]{3,2,1,0:T(4,128)(2,1)S(1)} %get-tuple-element.43), channel_id=1, source_target_pairs={{1,0},{2,1},{3,2},{0,3},{5,4},{6,5},{7,6},{4,7},{9,8},{10,9},{11,1... | collective-permute-start | bytes 368648 | tf_op jit(solution)/shard_map/ppermute | solution.py:19
  16.0 0.7 fusion.53
  16.7 0.3 reduce_window_sum.11
  16.9 0.7 add_select_fusion
  17.6 0.3 convert_reduce_fusion
  18.2 0.2 select_reduce_fusion
  18.4 0.8 convert_multiply_fusion
  19.2 0.8 gather_fusion.1
  20.2 0.9 %fusion.42 = f32[2,60,128]{2,1,0:T(8,128)S(1)} fusion(bf16[128,2,72]{0,2,1:T(8,128)(2,1)S(1)} %bitcast.56, f32[60,72]{1,0:T(8,128)} %param.11), kind=kOutput, calls=%fused_computation.79 | convolution fusion | flops 13286400 | bytes 115584 | tf_op jit(solution)/shard_map/sfm,lm->fls/dot_general | solution.py:80
  21.1 0.7 collective-permute-done.1
  21.8 1.1 %maximum_convert_fusion = f32[2,60,72,128]{3,2,1,0:T(8,128)S(1)} fusion(bf16[2,60,4,128]{3,2,1,0:T(4,128)(2,1)S(1)} %collective-permute-done.1, bf16[2,60,64,128]{3,2,1,0:T(8,128)(2,1)S(1)} %copy-done.2, bf16[2,60,4,128]{3,2,1,0:T(4,128)(2,1)S(1)} %collective-permute-done), kind=kLoop, calls=%fused_computation.67 | loop fusion | flops 6635520 | bytes 6635520 | tf_op jit(solution)/shard_map/convert_element_type | solution.py:83
  22.9 2.0 %fusion.14 = f32[2,60,70,128]{3,2,1,0:T(8,128)S(1)} fusion(f32[2,60,72,128]{3,2,1,0:T(8,128)S(1)} %maximum_convert_fusion, f32[60,128]{1,0:T(8,128)S(1)} %copy-done.4), kind=kLoop, calls=%fused_computation.33 | loop fusion | flops 8601600 | bytes 17233920 | tf_op jit(solution)/shard_map/add | solution.py:29
  24.9 0.6 fusion.60
  25.4 3.4 %fusion.18 = f32[2,60,70,128]{3,2,1,0:T(8,128)S(1)} fusion(f32[2,1,70,128]{3,2,1,0:T(8,128)S(1)} %get-tuple-element.33, f32[2,59,70,128]{3,2,1,0:T(8,128)S(1)} %get-tuple-element.35, f32[2,59,70,128]{3,2,1,0:T(8,128)S(1)} %get-tuple-element.34, f32[2,1,70,128]{3,2,1,0:T(8,128)S(1)} %get-tuple-element.32, f32[2,60,128]{2,1,0:T(8,128)S(1)} %fusion.42, ...), kind=kLoop, calls=%fused_computation.38 | loop fusion | flops 17203200 | bytes 25896960 | tf_op jit(solution)/shard_map/add | solution.py:39
  28.9 0.4 slice_add_fusion.2
  29.3 2.0 %fusion.11 = f32[2,60,68,128]{3,2,1,0:T(8,128)S(1)} fusion(f32[1,60,70,128]{3,2,1,0:T(8,128)S(1)} %get-tuple-element.23, f32[1,60,70,128]{3,2,1,0:T(8,128)S(1)} %get-tuple-element.22, f32[60,128]{1,0:T(8,128)S(1)} %copy-done.4), kind=kLoop, calls=%fused_computation.29 | loop fusion | flops 11489280 | bytes 8509440 | tf_op jit(solution)/shard_map/add | solution.py:29
  31.3 0.6 fusion.58
  31.9 3.6 %fusion.22 = f32[2,60,68,128]{3,2,1,0:T(8,128)S(1)} fusion(f32[2,1,68,128]{3,2,1,0:T(8,128)S(1)} %get-tuple-element.29, f32[2,59,68,128]{3,2,1,0:T(8,128)S(1)} %get-tuple-element.31, f32[2,59,68,128]{3,2,1,0:T(8,128)S(1)} %get-tuple-element.30, f32[2,1,68,128]{3,2,1,0:T(8,128)S(1)} %get-tuple-element.28, f32[2,60,128]{2,1,0:T(8,128)S(1)} %fusion.42, ...), kind=kLoop, calls=%fused_computation.43 | loop fusion | flops 19845120 | bytes 16926720 | tf_op jit(solution)/shard_map/add | solution.py:39
  35.5 0.4 slice_add_fusion.1
  35.9 2.0 %fusion.7 = f32[2,60,66,128]{3,2,1,0:T(8,128)S(1)} fusion(f32[1,60,68,128]{3,2,1,0:T(8,128)S(1)} %get-tuple-element.21, f32[1,60,68,128]{3,2,1,0:T(8,128)S(1)} %get-tuple-element.20, f32[60,128]{1,0:T(8,128)S(1)} %copy-done.4), kind=kLoop, calls=%fused_computation.24 | loop fusion | flops 11151360 | bytes 8263680 | tf_op jit(solution)/shard_map/add | solution.py:29
  37.9 0.6 fusion.56
  38.5 3.6 %fusion.26 = f32[2,60,66,128]{3,2,1,0:T(8,128)S(1)} fusion(f32[2,1,66,128]{3,2,1,0:T(8,128)S(1)} %get-tuple-element.25, f32[2,59,66,128]{3,2,1,0:T(8,128)S(1)} %get-tuple-element.27, f32[2,59,66,128]{3,2,1,0:T(8,128)S(1)} %get-tuple-element.26, f32[2,1,66,128]{3,2,1,0:T(8,128)S(1)} %get-tuple-element.24, f32[2,60,128]{2,1,0:T(8,128)S(1)} %fusion.42, ...), kind=kLoop, calls=%fused_computation.48 | loop fusion | flops 19261440 | bytes 16435200 | tf_op jit(solution)/shard_map/add | solution.py:39
  42.1 0.4 slice_add_fusion
  42.6 1.8 %fusion.32 = f32[2,60,64,128]{3,2,1,0:T(8,128)S(1)} fusion(f32[1,60,66,128]{3,2,1,0:T(8,128)S(1)} %get-tuple-element.19, f32[1,60,66,128]{3,2,1,0:T(8,128)S(1)} %get-tuple-element.18, f32[60,128]{1,0:T(8,128)S(1)} %copy-done.4), kind=kLoop, calls=%fused_computation.55 | loop fusion | flops 10813440 | bytes 8017920 | tf_op jit(solution)/shard_map/add | solution.py:29
  44.4 1.2 %fusion.62 = (f32[2,59,64,128]{3,2,1,0:T(8,128)S(1)}, f32[2,59,64,128]{3,2,1,0:T(8,128)S(1)}) fusion(f32[2,60,64,128]{3,2,1,0:T(8,128)S(1)} %fusion.32), kind=kLoop, calls=%fused_computation.133 | loop fusion | bytes 15466496 | tf_op jit(solution)/shard_map/slice | solution.py:37
  45.6 3.3 %fusion.36 = f32[2,60,64,128]{3,2,1,0:T(8,128)S(1)} fusion(f32[2,1,64,128]{3,2,1,0:T(8,128)S(1)} %get-tuple-element.39, f32[2,59,64,128]{3,2,1,0:T(8,128)S(1)} %get-tuple-element.41, f32[2,59,64,128]{3,2,1,0:T(8,128)S(1)} %get-tuple-element.40, f32[2,1,64,128]{3,2,1,0:T(8,128)S(1)} %get-tuple-element.38, f32[2,60,128]{2,1,0:T(8,128)S(1)} %fusion.42, ...), kind=kLoop, calls=%fused_computation.60 | loop fusion | flops 18677760 | bytes 15943680 | tf_op jit(solution)/shard_map/add | solution.py:39
  49.0 0.6 slice_add_fusion.3
  49.6 1.3 %copy-done.1 = f32[1,60,64,128]{3,2,1,0:T(8,128)} copy-done((f32[1,60,64,128]{3,2,1,0:T(8,128)}, f32[1,60,64,128]{3,2,1,0:T(8,128)S(1)}, u32[]{:S(2)}) %copy-start.1) | copy-done | bytes 1966104
  50.9 0.9 %subtract_reduce_fusion = f32[2,60,128]{2,1,0:T(8,128)S(1)} fusion(bf16[2,60,64,128]{3,2,1,0:T(8,128)(2,1)S(1)} %copy-done.3, f32[1,60,64,128]{3,2,1,0:T(8,128)S(1)} %get-tuple-element.37, f32[1,60,64,128]{3,2,1,0:T(8,128)S(1)} %get-tuple-element.36), kind=kLoop, calls=%fused_computation.62 | loop fusion | flops 3916800 | bytes 5959680 | tf_op jit(solution)/shard_map/reduce_sum | solution.py:87
  51.9 0.3 convolution_multiply_fusion
  52.2 20.0 %psum.7 = bf16[128,144]{1,0:T(8,128)(2,1)S(1)} all-reduce(f32[128,144]{1,0:T(8,128)S(1)} %copy.23), channel_id=1, replica_groups=mesh['wide'=8,'narrow'=4] {'narrow'}, use_global_device_ids=true, to_apply=%region_8.9 | all-reduce | flops 18432 | bytes 110592 | tf_op jit(solution)/shard_map/psum | solution.py:92
  72.2 1.8 %gather_fusion.2 = bf16[256,144]{1,0:T(8,128)(2,1)} fusion(bf16[128,144]{1,0:T(8,128)(2,1)S(1)} %psum.7, s32[1024]{0:T(1024)S(1)} %pad_clamp_fusion.1), kind=kCustom, calls=%fused_computation.2 | custom fusion | bytes 148480 | tf_op jit(solution)/shard_map/gather | solution.py:94
  74.0 3.8 %all-to-all-start.1 = ((bf16[8,32,144]{2,1,0:T(8,128)(2,1)}), bf16[8,32,144]{2,1,0:T(8,128)(2,1)S(1)}, u32[]{:S(2)}, u32[]{:S(2)}) async-start(bf16[8,32,144]{2,1,0:T(8,128)(2,1)} %bitcast.14), calls=%async_computation.1 | async-start | bytes 262144 | tf_op jit(solution)/shard_map/all_to_all | solution.py:93
  77.8 3.1 %fusion.37 = bf16[2,60,64,128]{3,2,1,0:T(8,128)(2,1)} fusion(f32[1,60,64,128]{3,2,1,0:T(8,128)} %copy-done.1, f32[1,60,64,128]{3,2,1,0:T(8,128)S(1)} %get-tuple-element.36), kind=kLoop, calls=%fused_computation.63 | loop fusion | flops 983040 | bytes 5898240 | tf_op jit(solution)/shard_map/convert_element_type | solution.py:86
  81.0 2.4 %all-to-all-done.1 = bf16[8,32,144]{2,1,0:T(8,128)(2,1)S(1)} async-done(((bf16[8,32,144]{2,1,0:T(8,128)(2,1)}), bf16[8,32,144]{2,1,0:T(8,128)(2,1)S(1)}, u32[]{:S(2)}, u32[]{:S(2)}) %all-to-all-start.1) | async-done | bytes 73760 | tf_op jit(solution)/shard_map/all_to_all | solution.py:93
  83.4 0.8 gather_fusion.3
  84.2 0.7 copy.24
  (30 shorter events, 0.7 us)
Async XLA Ops:
  0.6 51.2 %copy-start = (f32[72,60]{0,1:T(8,128)S(1)}, f32[72,60]{0,1:T(8,128)}, u32[]{:S(2)}) copy-start(f32[72,60]{0,1:T(8,128)} %param.12) | copy-start | bytes 51844
  0.6 21.2 %copy-start.2 = (bf16[2,60,64,128]{3,2,1,0:T(8,128)(2,1)S(1)}, bf16[2,60,64,128]{3,2,1,0:T(8,128)(2,1)}, u32[]{:S(2)}) copy-start(bf16[2,60,64,128]{3,2,1,0:T(8,128)(2,1)} %param.8) | copy-start | bytes 5898244
  5.0 17.9 %copy-start.4 = (f32[60,128]{1,0:T(8,128)S(1)}, f32[60,128]{1,0:T(8,128)}, u32[]{:S(2)}) copy-start(f32[60,128]{1,0:T(8,128)} %param.9) | copy-start | bytes 92164
  5.7 13.5 %all-to-all-start = ((bf16[8,32,144]{2,1,0:T(8,128)(2,1)}), bf16[8,32,144]{2,1,0:T(8,128)(2,1)S(1)}, u32[]{:S(2)}, u32[]{:S(2)}) async-start(bf16[8,32,144]{2,1,0:T(8,128)(2,1)} %broadcast_select_fusion), calls=%async_computation | async-start | bytes 262144 | tf_op jit(solution)/shard_map/all_to_all | solution.py:78
  12.1 9.0 %collective-permute-start = (bf16[2,60,4,128]{3,2,1,0:T(4,128)(2,1)S(1)}, bf16[2,60,4,128]{3,2,1,0:T(4,128)(2,1)S(1)}, u32[]{:S(2)}, u32[]{:S(2)}) collective-permute-start(bf16[2,60,4,128]{3,2,1,0:T(4,128)(2,1)S(1)} %get-tuple-element.42), channel_id=1, source_target_pairs={{0,1},{1,2},{2,3},{3,0},{4,5},{5,6},{6,7},{7,4},{8,9},{9,10},{10,1... | collective-permute-start | bytes 368648 | tf_op jit(solution)/shard_map/ppermute | solution.py:16
  13.7 8.1 %collective-permute-start.1 = (bf16[2,60,4,128]{3,2,1,0:T(4,128)(2,1)S(1)}, bf16[2,60,4,128]{3,2,1,0:T(4,128)(2,1)S(1)}, u32[]{:S(2)}, u32[]{:S(2)}) collective-permute-start(bf16[2,60,4,128]{3,2,1,0:T(4,128)(2,1)S(1)} %get-tuple-element.43), channel_id=1, source_target_pairs={{1,0},{2,1},{3,2},{0,3},{5,4},{6,5},{7,6},{4,7},{9,8},{10,9},{11,1... | collective-permute-start | bytes 368648 | tf_op jit(solution)/shard_map/ppermute | solution.py:19
  49.0 1.9 %copy-start.3 = (bf16[2,60,64,128]{3,2,1,0:T(8,128)(2,1)S(1)}, bf16[2,60,64,128]{3,2,1,0:T(8,128)(2,1)}, u32[]{:S(2)}) copy-start(bf16[2,60,64,128]{3,2,1,0:T(8,128)(2,1)} %param.8) | copy-start | bytes 5898244
  49.6 1.3 %copy-start.1 = (f32[1,60,64,128]{3,2,1,0:T(8,128)}, f32[1,60,64,128]{3,2,1,0:T(8,128)S(1)}, u32[]{:S(2)}) copy-start(f32[1,60,64,128]{3,2,1,0:T(8,128)S(1)} %get-tuple-element.37) | copy-start | bytes 5898244
  74.0 9.3 %all-to-all-start.1 = ((bf16[8,32,144]{2,1,0:T(8,128)(2,1)}), bf16[8,32,144]{2,1,0:T(8,128)(2,1)S(1)}, u32[]{:S(2)}, u32[]{:S(2)}) async-start(bf16[8,32,144]{2,1,0:T(8,128)(2,1)} %bitcast.14), calls=%async_computation.1 | async-start | bytes 262144 | tf_op jit(solution)/shard_map/all_to_all | solution.py:93
where the time goes:
time: 85.6 us; the launch traced here: 84.9 us
  other arithmetic  35.4 us (41%)
  blocking collectives  20 us (23%)
  starting transfers between devices  12.8 us (15%)
  local copies, waits for them, and re-layouts  11.4 us (13%)
  waiting for transfers between devices  3.07 us (4%)
  matrix products  1.19 us (1%)
  between operations  0.98 us (1%)
    psum x1, blocking collectives, shards(): totals = lax.psum(partial_term, 'narrow').astype(jnp.bfloat16)  20 us
    add x4, other arithmetic, column_physics(): fields = fields + 0.25 * forcing[:, :, None, :]  14 us
    add x4, other arithmetic, horizontal(): middle + courant_now[None, :, None, :] * (left_cells - middle)  7.74 us
    all_to_all x1, starting transfers between devices, shards(): lax.all_to_all(packed, 'wide', split_axis=0, concat_axis=0, tiled=True)  5.17 us
    all_to_all x1, starting transfers between devices, shards(): lax.all_to_all(totals[slot_of_buffer], 'wide', split_axis=0, concat_axis=...  3.8 us
    convert_element_type x1, other arithmetic, shards(): crm_new = fields.astype(jnp.bfloat16)  3.14 us
    slice x8, local copies, waits for them, and re-layouts, column_physics(): below_cells = jnp.concatenate([fields[:, :1], fields[:, :-1]], axis=1)  2.95 us
    all_to_all x1, waiting for transfers between devices, shards(): lax.all_to_all(totals[slot_of_buffer], 'wide', split_axis=0, concat_axis=...  2.39 us
  transfers between devices with their start and end apart: 4, of which 2 were waited for; matrix products, arithmetic and copies ran while one was open for 11% of the time, Pallas kernels for 0%

commit v1 on v0

v1 whole, which is shorter than its diff:
```python
import functools

import jax
import jax.numpy as jnp
from jax import lax
from jax.experimental import pallas as pl
from jax.experimental.pallas import tpu as pltpu
from jax.sharding import PartitionSpec as P

SUB = 4
MESH = pl.DeviceIdType.MESH
EXACT = lax.Precision.HIGHEST
SCALE = 0.015


def on_rows(ref, start, size):
    return ref.at[pl.ds(pl.multiple_of(start, size), size)]


def greet(axes):
    barrier = pltpu.get_barrier_semaphore()
    count = 0
    for axis, steps in axes:
        size = lax.axis_size(axis)
        me = lax.axis_index(axis)
        for step in steps:
            pl.semaphore_signal(
                barrier, inc=1, device_id={axis: lax.rem(me + step, size)}, device_id_type=MESH
            )
            count += 1
    pl.semaphore_wait(barrier, count)


def peers(axis, source, place, send_sem, recv_sem):
    size = lax.axis_size(axis)
    me = lax.axis_index(axis)
    out, arriving = [], []
    for step in range(1, size):
        target = lax.rem(me + step, size)
        origin = lax.rem(me + size - step, size)
        out.append(
            pltpu.make_async_remote_copy(
                src_ref=source(target),
                dst_ref=place(me),
                send_sem=send_sem.at[step],
                recv_sem=recv_sem.at[me],
                device_id={axis: target},
                device_id_type=MESH,
            )
        )
        arriving.append(
            pltpu.make_async_remote_copy(
                src_ref=source(target),
                dst_ref=place(origin),
                send_sem=send_sem.at[step],
                recv_sem=recv_sem.at[origin],
                device_id={axis: target},
                device_id_type=MESH,
            )
        )
    return out, arriving


def send_kernel(
    slots_ref, gcm_ref, down_ref, crm_ref,
    low_ref, high_ref, forcing_ref, place_ref, pick_ref,
    top, bottom, top_out, bottom_out, packed, landed, ranks,
    local_sem, send_sem, recv_sem, halo_send, halo_recv,
):
    wide = lax.axis_size("wide")
    narrow = lax.axis_size("narrow")
    me = lax.axis_index("wide")
    depth = lax.axis_index("narrow")
    columns = gcm_ref.shape[0]
    rows = packed.shape[0] // wide
    levels, cells = crm_ref.shape[1], crm_ref.shape[2]
    top_copy = pltpu.make_async_copy(crm_ref.at[:, :, 0:16, :], top, local_sem.at[0])
    bottom_copy = pltpu.make_async_copy(
        crm_ref.at[:, :, cells - 16 : cells, :], bottom, local_sem.at[1]
    )
    top_copy.start()
    bottom_copy.start()
    greet((("wide", range(1, wide)), ("narrow", (1, narrow - 1))))

    mine = slots_ref[pl.ds(me, 1), :]
    owner_first = lax.broadcasted_iota(jnp.int32, (wide, columns), 0) * columns
    goes = (mine >= owner_first) & (mine < owner_first + columns)
    before = (
        lax.broadcasted_iota(jnp.int32, (columns, columns), 0)
        < lax.broadcasted_iota(jnp.int32, (columns, columns), 1)
    ).astype(jnp.float32).astype(jnp.bfloat16)

    def ranked(member):
        member = member.astype(jnp.float32)
        order = jnp.dot(member.astype(jnp.bfloat16), before, preferred_element_type=jnp.float32)
        return jnp.where(member > 0.0, order, -1.0)

    within = lax.broadcasted_iota(jnp.int32, (rows, columns), 0).astype(jnp.float32)
    ranks[...] = ranked(goes)
    for target in range(wide):
        hit = (ranks[target : target + 1, :] == within).astype(jnp.float32).astype(jnp.bfloat16)
        pick_ref[target * rows : (target + 1) * rows, :] = hit
    sent = gcm_ref[...].astype(jnp.bfloat16)
    packed[...] = jnp.dot(pick_ref[...], sent, preferred_element_type=jnp.float32).astype(
        jnp.bfloat16
    )
    states, states_in = peers(
        "wide",
        lambda target: on_rows(packed, target * rows, rows),
        lambda origin: on_rows(landed, origin * rows, rows),
        send_sem,
        recv_sem,
    )
    for copy in states:
        copy.start()
    own_rows = pl.ds(pl.multiple_of(me * rows, rows), rows)
    landed[own_rows, :] = packed[own_rows, :]

    first_half = lax.broadcasted_iota(jnp.int32, (8, columns), 0) < 4
    top_copy.wait()
    bottom_copy.wait()
    for field in range(2):

        def gather(group, carry):
            low_parts, high_parts = [], []
            for pair in range(2):
                level = group * 4 + pair * 2
                a = top[field, level].astype(jnp.float32)[0:8]
                b = top[field, level + 1].astype(jnp.float32)[0:8]
                low_parts.append(jnp.where(first_half, a, pltpu.roll(b, 4, 0)))
                a = bottom[field, level].astype(jnp.float32)[8:16]
                b = bottom[field, level + 1].astype(jnp.float32)[8:16]
                high_parts.append(jnp.where(first_half, pltpu.roll(a, 4, 0), b))
            at = pl.ds(pl.multiple_of(field * levels * 4 + group * 16, 16), 16)
            top_out[at, :] = jnp.concatenate(low_parts, axis=0).astype(jnp.bfloat16)
            bottom_out[at, :] = jnp.concatenate(high_parts, axis=0).astype(jnp.bfloat16)
            return carry

        lax.fori_loop(0, levels // 4, gather, 0)

    def halo(source, dest, which, step):
        return pltpu.make_async_remote_copy(
            src_ref=source,
            dst_ref=dest,
            send_sem=halo_send.at[which],
            recv_sem=halo_recv.at[which],
            device_id={"narrow": lax.rem(depth + step, narrow)},
            device_id_type=MESH,
        )

    onward = halo(bottom_out, low_ref, 0, 1)
    backward = halo(top_out, high_ref, 1, narrow - 1)
    onward.start()
    backward.start()

    first = me * columns
    slots = slots_ref[...]
    ranks[...] = ranked((slots >= first) & (slots < first + columns))
    slot_number = lax.broadcasted_iota(jnp.int32, (columns, columns), 0) + first
    for origin in range(wide):
        hit = (ranks[origin : origin + 1, :] == within).astype(jnp.float32).astype(jnp.bfloat16)
        spot = (slots_ref[origin : origin + 1, :] == slot_number).astype(jnp.float32)
        place_ref[origin * rows : (origin + 1) * rows, :] = lax.dot_general(
            hit,
            spot.astype(jnp.bfloat16),
            (((1,), (1,)), ((), ())),
            preferred_element_type=jnp.float32,
        ).astype(jnp.bfloat16)
    for copy in states_in:
        copy.wait_recv()
    by_slot = lax.dot_general(
        landed[...],
        place_ref[...],
        (((0,), (0,)), ((), ())),
        preferred_element_type=jnp.float32,
    )
    span = by_slot.shape[0] // 2
    for field in range(2):
        forcing_ref[field] = jnp.dot(
            down_ref[...],
            by_slot[field * span : (field + 1) * span],
            precision=EXACT,
            preferred_element_type=jnp.float32,
        )
    for copy in states:
        copy.wait_send()
    onward.wait()
    backward.wait()


def physics_kernel(
    crm_ref, low_ref, high_ref, forcing_ref, courant_ref, cloud_ref,
    out_ref, change_ref,
    slab, state, left_gain, middle_gain, keep, push,
):
    levels, cells = crm_ref.shape[1], crm_ref.shape[2]
    parts = (cells + 2 * SUB) // 8
    courant = courant_ref[...]
    left_gain[...] = (courant + 0.15) * (1.0 / 0.15)
    middle_gain[...] = (0.7 - courant) * (1.0 / 0.15)
    keep[...] = 1.0 - 0.3 * cloud_ref[...].astype(jnp.float32)
    for substep in range(SUB):
        gain = 0.25 / SCALE ** (substep + 1)
        push[2 * substep + 1] = gain * forcing_ref[1]
        push[2 * substep] = gain * (forcing_ref[0] + 2.0 * forcing_ref[1])

    for field in range(2):

        def spread(group, carry):
            at = pl.ds(pl.multiple_of(field * levels * 4 + group * 16, 16), 16)
            low = low_ref[at, :].astype(jnp.float32)
            high = high_ref[at, :].astype(jnp.float32)
            for step in range(4):
                level = group * 4 + step
                from_row = 8 * (step // 2)
                low_part = low[from_row : from_row + 8]
                high_part = high[from_row : from_row + 8]
                if step % 2 == 0:
                    low_part = pltpu.roll(low_part, 4, 0)
                else:
                    high_part = pltpu.roll(high_part, 4, 0)
                slab[field * levels + level, 0:8, :] = low_part
                slab[field * levels + level, cells + 8 : cells + 16, :] = high_part
                slab[field * levels + level, 8 : cells + 8, :] = crm_ref[field, level].astype(
                    jnp.float32
                )
            return carry

        lax.fori_loop(0, levels // 4, spread, 0)

    def strided(field, level, part):
        return slab[field * levels + level, pl.ds(4 + part, 8, stride=parts), :]

    for substep in range(SUB):
        for field in (1, 0):

            def fetch(level):
                if substep > 0:
                    return [state[field * levels + level, part] for part in range(parts)]
                moist = [strided(1, level, part) for part in range(parts)]
                if field == 1:
                    return moist
                return [strided(0, level, part) + 2.0 * moist[part] for part in range(parts)]

            def across(level):
                cell = fetch(level)
                gain_left = left_gain[pl.ds(level, 1), :]
                gain_middle = middle_gain[pl.ds(level, 1), :]
                before = [pltpu.roll(cell[-1], 1, 0)] + cell[:-1]
                after = cell[1:] + [pltpu.roll(cell[0], 7, 0)]
                return [
                    after[part] + gain_left * before[part] + gain_middle * cell[part]
                    for part in range(parts)
                ]

            def finish(level, below, here, above):
                forced = push[2 * substep + field, pl.ds(level, 1), :]
                kept = keep[pl.ds(level, 1), :]
                for part in range(parts):
                    value = (below[part] + above[part]) + (8.0 * here[part] + forced)
                    if field == 1:
                        value = jnp.minimum(value, kept * value)
                    if substep == SUB - 1:
                        value = value * (SCALE**SUB)
                        if field == 1:
                            state[levels + level, part] = value
                        else:
                            value = value - 2.0 * state[levels + level, part]
                        slab[
                            field * levels + level, pl.ds(4 + part, 8, stride=parts), :
                        ] = value
                    else:
                        state[field * levels + level, part] = value

            def climb(level, carry):
                below, here = carry
                above = across(level + 1)
                finish(level, below, here, above)
                return here, above

            first = across(0)
            second = across(1)
            finish(0, first, first, second)
            below, here = lax.fori_loop(1, levels - 1, climb, (first, second), unroll=2)
            finish(levels - 1, below, here, here)

    for field in range(2):

        def close(level, carry):
            final = slab[field * levels + level, 8 : cells + 8, :]
            out_ref[field, level] = final.astype(jnp.bfloat16)
            moved = final - crm_ref[field, level].astype(jnp.float32)
            change_ref[field, pl.ds(level, 1), :] = jnp.sum(moved, axis=0, keepdims=True)
            return carry

        lax.fori_loop(0, levels, close, 0, unroll=2)


def return_kernel(
    share, change_ref, up_ref, place_ref, pick_ref,
    out_ref,
    sums, packed, landed,
    sum_send, sum_recv, send_sem, recv_sem,
):
    wide = lax.axis_size("wide")
    narrow = lax.axis_size("narrow")
    me = lax.axis_index("wide")
    depth = lax.axis_index("narrow")
    rows = packed.shape[0] // wide
    greet((("wide", range(1, wide)), ("narrow", range(1, narrow))))
    partial, partial_in = peers(
        "narrow", lambda target: change_ref, lambda origin: sums.at[origin], sum_send, sum_recv
    )
    for copy in partial:
        copy.start()
    sums[depth] = change_ref[...]
    for copy in partial_in:
        copy.wait_recv()
    total = sums[0]
    for origin in range(1, narrow):
        total = total + sums[origin]
    tendency = jnp.concatenate(
        [
            jnp.dot(
                up_ref[...], total[field], precision=EXACT, preferred_element_type=jnp.float32
            )
            for field in range(2)
        ],
        axis=0,
    )
    tendency = (tendency * share).astype(jnp.bfloat16)
    packed[...] = lax.dot_general(
        place_ref[...], tendency, (((1,), (1,)), ((), ())), preferred_element_type=jnp.float32
    ).astype(jnp.bfloat16)
    back, back_in = peers(
        "wide",
        lambda target: on_rows(packed, target * rows, rows),
        lambda origin: on_rows(landed, origin * rows, rows),
        send_sem,
        recv_sem,
    )
    for copy in back:
        copy.start()
    own_rows = pl.ds(pl.multiple_of(me * rows, rows), rows)
    landed[own_rows, :] = packed[own_rows, :]
    for copy in back_in:
        copy.wait_recv()
    out_ref[...] = lax.dot_general(
        pick_ref[...], landed[...], (((0,), (0,)), ((), ())), preferred_element_type=jnp.float32
    ).astype(jnp.bfloat16)
    for copy in partial + back:
        copy.wait_send()


def shards(gcm_state, crm_state, courant, cloud_mask, level_down, level_up, column_map):
    wide = lax.axis_size("wide")
    narrow = lax.axis_size("narrow")
    columns, width = gcm_state.shape
    _, levels, cells, _ = crm_state.shape
    capacity = -(-2 * columns // wide)
    rows = -(-capacity // 16) * 16
    total = wide * rows
    halo = 2 * levels * SUB
    vmem = pl.BlockSpec(memory_space=pltpu.VMEM)
    struct = jax.ShapeDtypeStruct
    dma = pltpu.SemaphoreType.DMA
    low, high, forcing, place, pick = pl.pallas_call(
        send_kernel,
        out_shape=(
            struct((halo, columns), jnp.bfloat16),
            struct((halo, columns), jnp.bfloat16),
            struct((2, levels, columns), jnp.float32),
            struct((total, columns), jnp.bfloat16),
            struct((total, columns), jnp.bfloat16),
        ),
        in_specs=[vmem, vmem, vmem, pl.BlockSpec(memory_space=pl.ANY)],
        out_specs=(vmem,) * 5,
        scratch_shapes=[
            pltpu.VMEM((2, levels, 16, columns), jnp.bfloat16),
            pltpu.VMEM((2, levels, 16, columns), jnp.bfloat16),
            pltpu.VMEM((halo, columns), jnp.bfloat16),
            pltpu.VMEM((halo, columns), jnp.bfloat16),
            pltpu.VMEM((total, width), jnp.bfloat16),
            pltpu.VMEM((total, width), jnp.bfloat16),
            pltpu.VMEM((wide, columns), jnp.float32),
            dma((2,)),
            dma((wide,)),
            dma((wide,)),
            dma((2,)),
            dma((2,)),
        ],
        compiler_params=pltpu.CompilerParams(
            collective_id=0, has_side_effects=True, vmem_limit_bytes=24 * 2**20
        ),
        name="send",
    )(column_map.reshape(wide, columns), gcm_state, level_down, crm_state)
    crm_new, change = pl.pallas_call(
        physics_kernel,
        out_shape=(
            struct(crm_state.shape, jnp.bfloat16),
            struct((2, levels, columns), jnp.float32),
        ),
        in_specs=[vmem] * 6,
        out_specs=(vmem,) * 2,
        scratch_shapes=[
            pltpu.VMEM((2 * levels, cells + 16, columns), jnp.float32),
            pltpu.VMEM((2 * levels, (cells + 2 * SUB) // 8, 8, columns), jnp.float32),
            pltpu.VMEM((levels, columns), jnp.float32),
            pltpu.VMEM((levels, columns), jnp.float32),
            pltpu.VMEM((levels, columns), jnp.float32),
            pltpu.VMEM((2 * SUB, levels, columns), jnp.float32),
        ],
        compiler_params=pltpu.CompilerParams(vmem_limit_bytes=32 * 2**20),
        name="physics",
    )(crm_state, low, high, forcing, courant, cloud_mask)
    gcm_tendency = pl.pallas_call(
        functools.partial(return_kernel, 1.0 / (cells * narrow * SUB)),
        out_shape=struct((columns, width), jnp.bfloat16),
        in_specs=[vmem] * 4,
        out_specs=vmem,
        scratch_shapes=[
            pltpu.VMEM((narrow, 2, levels, columns), jnp.float32),
            pltpu.VMEM((total, width), jnp.bfloat16),
            pltpu.VMEM((total, width), jnp.bfloat16),
            dma((narrow,)),
            dma((narrow,)),
            dma((wide,)),
            dma((wide,)),
        ],
        compiler_params=pltpu.CompilerParams(
            collective_id=1, has_side_effects=True, vmem_limit_bytes=24 * 2**20
        ),
        name="back",
    )(change, level_up, place, pick)
    return gcm_tendency, crm_new


def solution(mesh):
    placed = (
        P("wide", None),
        P(None, None, "narrow", "wide"),
        P(None, "wide"),
        P(None, "wide"),
        P(),
        P(),
        P(),
    )
    return jax.shard_map(
        shards,
        mesh=mesh,
        in_specs=placed,
        out_specs=(P("wide", None), P(None, None, "narrow", "wide")),
        check_vma=False,
    )
```

time: 85.6 us -> 42.3 us (0.49)
  Pallas kernels: 0 us -> 36.5 us
  other arithmetic: 35.4 us -> 0 us
  blocking collectives: 20 us -> 0 us
  starting transfers between devices: 12.8 us -> 0 us
  local copies, waits for them, and re-layouts: 11.4 us -> 4.79 us
  waiting for transfers between devices: 3.07 us -> 0 us
  matrix products: 1.19 us -> 0 us
    pallas_call x0 -> x3, Pallas kernels: none -> 36.5 us  [the longest x1 13.5 us: shards(): pl.pallas_call(functools.partial(return_kernel, 1.0 / (cells * narrow * S...]
    add x12 -> x0, other arithmetic: 23.6 us -> none  [the longest x4 14 us: column_physics(): fields = fields + 0.25 * forcing[:, :, None, :]]
    psum x1 -> x0, blocking collectives: 20 us -> none  [shards(): totals = lax.psum(partial_term, 'narrow').astype(jnp.bfloat16)]
    all_to_all x2 -> x0, starting transfers between devices: 8.97 us -> none  [the longest x1 5.17 us: shards(): lax.all_to_all(packed, 'wide', split_axis=0, concat_axis=0, tiled=True)]
    convert_element_type x4 -> x0, other arithmetic: 5.79 us -> none  [the longest x1 3.14 us: shards(): crm_new = fields.astype(jnp.bfloat16)]
    gather x5 -> x0, local copies, waits for them, and re-layouts: 4.74 us -> none  [the longest x1 1.79 us: shards(): totals[slot_of_buffer]]
    slice x9 -> x0, local copies, waits for them, and re-layouts: 4.12 us -> none  [the longest x8 2.95 us: column_physics(): below_cells = jnp.concatenate([fields[:, :1], fields[:, :-1]], axis=1)]
    ppermute x2 -> x0, starting transfers between devices: 3.88 us -> none  [the longest x1 2.25 us: with_halo(): lax.ppermute(lax.slice_in_dim(block, 0, width, axis=dim), axis, backward)]
  transfers between devices with their start and end apart: 4 -> 0, of which waited for: 2 -> 0; matrix products, arithmetic and copies ran while one was open for 11% -> 0% of each run, Pallas kernels for 0% -> 0%
where the time goes in v1:
time: 42.3 us; the launch traced here: 42 us
  Pallas kernels  36.5 us (86%)
  local copies, waits for them, and re-layouts  4.79 us (11%)
  between operations  0.71 us (2%)
    pallas_call x1, Pallas kernels, shards(): pl.pallas_call(functools.partial(return_kernel, 1.0 / (cells * narrow * S...  13.5 us
    pallas_call x1, Pallas kernels, shards(): pl.pallas_call(send_kernel, out_shape=(struct((halo, columns), jnp.bfloat...  12.7 us
    pallas_call x1, Pallas kernels, shards(): pl.pallas_call(physics_kernel, out_shape=(struct(crm_state.shape, jnp.bfl...  10.3 us
    unnamed x17, local copies, waits for them, and re-layouts  4.79 us

profile of v1, /device:TPU:0, one launch (start us, length us, event | category | flops | bytes accessed | tf_op | source)
XLA Modules:
  0.0 42.0 jit_solution(10178087053904844237)
XLA Ops:
  0.6 0.0 copy-start.4
  0.6 0.0 copy-start.3
  0.6 1.0 %copy.9.gcm_ref = f32[128,144]{1,0:T(8,128)S(1)} copy(f32[128,144]{0,1:T(8,128)} %param.7) | data formatting | bytes 147456 | tf_op args[0]
  1.6 0.0 copy-start
  1.7 1.5 %copy-done = bf16[2,60,64,128]{3,2,1,0:T(8,128)(2,1)S(1)} copy-done((bf16[2,60,64,128]{3,2,1,0:T(8,128)(2,1)S(1)}, bf16[2,60,64,128]{3,2,1,0:T(8,128)(2,1)}, u32[]{:S(2)}) %copy-start) | copy-done | bytes 1966104
  3.2 0.0 copy-start.2
  3.2 0.8 %copy-done.2 = f32[60,72]{1,0:T(8,128)S(1)} copy-done((f32[60,72]{1,0:T(8,128)S(1)}, f32[60,72]{1,0:T(8,128)}, u32[]{:S(2)}) %copy-start.2) | copy-done | bytes 17304
  4.0 0.0 copy-start.5
  4.0 0.7 %copy-done.5 = s32[1024]{0:T(1024)S(1)} copy-done((s32[1024]{0:T(1024)S(1)}, s32[1024]{0:T(1024)}, u32[]{:S(2)}) %copy-start.5) | copy-done | bytes 4120
  4.6 0.0 copy-start.1
  4.6 0.0 copy-start.6
  4.6 12.7 %send.1 = (bf16[480,128]{1,0:T(8,128)(2,1)S(1)}, bf16[480,128]{1,0:T(8,128)(2,1)S(1)}, f32[2,60,128]{2,1,0:T(8,128)S(1)}, bf16[256,128]{1,0:T(8,128)(2,1)S(1)}, bf16[256,128]{1,0:T(8,128)(2,1)S(1)}) custom-call(s32[8,128]{1,0:T(8,128)S(1)} %bitcast.1, f32[128,144]{1,0:T(8,128)S(1)} %copy.9.gcm_ref, f32[60,72]{1,0:T(8,128)S(1)} %copy-done.2, ...), custom_call_target="tpu_custom_call" | custom-call | tf_op jit(solution)/shard_map/send/pallas_call | solution.py:367
  17.3 0.0 copy-done.4
  17.4 0.0 copy-done.3
  17.4 0.0 copy-done.1
  17.4 10.3 %physics.1 = (bf16[2,60,64,128]{3,2,1,0:T(8,128)(2,1)}, f32[2,60,128]{2,1,0:T(8,128)S(1)}) custom-call(bf16[2,60,64,128]{3,2,1,0:T(8,128)(2,1)S(1)} %copy-done.1, bf16[480,128]{1,0:T(8,128)(2,1)S(1)} %get-tuple-element.9.low_ref, bf16[480,128]{1,0:T(8,128)(2,1)S(1)} %get-tuple-element.10.high_ref, f32[2,60,128]{2,1,0:T(8,128)S(1)} %get-tuple-element.11.forcing_ref, ...), custom_call_target="tpu_custom_call" | custom-call | tf_op jit(solution)/shard_map/physics/pallas_call | solution.py:397
  27.6 0.0 copy-done.6
  27.6 0.1 copy.10.up_ref
  27.7 13.5 %back.1 = bf16[128,144]{1,0:T(8,128)(2,1)S(1)} custom-call(f32[2,60,128]{2,1,0:T(8,128)S(1)} %get-tuple-element.12.change_ref, f32[72,60]{1,0:T(8,128)S(1)} %copy.10.up_ref, bf16[256,128]{1,0:T(8,128)(2,1)S(1)} %get-tuple-element.13.place_ref, bf16[256,128]{1,0:T(8,128)(2,1)S(1)} %get-tuple-element.14.pick_ref), custom_call_target="tpu_custom_call" | custom-call | tf_op jit(solution)/shard_map/back/pallas_call | solution.py:416
  41.3 0.7 %copy.11 = bf16[128,144]{0,1:T(8,128)(2,1)} copy(bf16[128,144]{1,0:T(8,128)(2,1)S(1)} %back.1) | data formatting | bytes 73728
Async XLA Ops:
  0.6 16.7 %copy-start.4 = (s32[60,128]{1,0:T(8,128)S(1)}, s32[60,128]{1,0:T(8,128)}, u32[]{:S(2)}) copy-start(s32[60,128]{1,0:T(8,128)} %cloud_ref.1) | copy-start | bytes 92164
  0.6 16.7 %copy-start.3 = (f32[60,128]{1,0:T(8,128)S(1)}, f32[60,128]{1,0:T(8,128)}, u32[]{:S(2)}) copy-start(f32[60,128]{1,0:T(8,128)} %courant_ref.1) | copy-start | bytes 92164
  1.6 1.5 %copy-start = (bf16[2,60,64,128]{3,2,1,0:T(8,128)(2,1)S(1)}, bf16[2,60,64,128]{3,2,1,0:T(8,128)(2,1)}, u32[]{:S(2)}) copy-start(bf16[2,60,64,128]{3,2,1,0:T(8,128)(2,1)} %crm_ref.3) | copy-start | bytes 5898244
  3.2 0.8 %copy-start.2 = (f32[60,72]{1,0:T(8,128)S(1)}, f32[60,72]{1,0:T(8,128)}, u32[]{:S(2)}) copy-start(f32[60,72]{1,0:T(8,128)} %down_ref.1) | copy-start | bytes 51844
  4.0 0.7 %copy-start.5 = (s32[1024]{0:T(1024)S(1)}, s32[1024]{0:T(1024)}, u32[]{:S(2)}) copy-start(s32[1024]{0:T(1024)} %param.13) | copy-start | bytes 12292
  4.6 12.7 %copy-start.1 = (bf16[2,60,64,128]{3,2,1,0:T(8,128)(2,1)S(1)}, bf16[2,60,64,128]{3,2,1,0:T(8,128)(2,1)}, u32[]{:S(2)}) copy-start(bf16[2,60,64,128]{3,2,1,0:T(8,128)(2,1)} %crm_ref.3) | copy-start | bytes 5898244
  4.6 23.0 %copy-start.6 = (f32[72,60]{0,1:T(8,128)S(1)}, f32[72,60]{0,1:T(8,128)}, u32[]{:S(2)}) copy-start(f32[72,60]{0,1:T(8,128)} %param.12) | copy-start | bytes 51844

commit v2 on v0

v2 whole, which is shorter than its diff:
```python
import jax
import jax.numpy as jnp
from jax import lax
from jax.experimental import pallas as pl
from jax.experimental.pallas import tpu as pltpu
from jax.sharding import PartitionSpec as P

SUB = 4
MESH = pl.DeviceIdType.MESH
EXACT = lax.Precision.HIGHEST
SCALE = 0.015


def on_rows(ref, start, size):
    return ref.at[pl.ds(pl.multiple_of(start, size), size)]


def peers(axis, source, place, send_sem, recv_sem):
    size = lax.axis_size(axis)
    me = lax.axis_index(axis)
    out, arriving = [], []
    for step in range(1, size):
        target = lax.rem(me + step, size)
        origin = lax.rem(me + size - step, size)
        out.append(
            pltpu.make_async_remote_copy(
                src_ref=source(target),
                dst_ref=place(me),
                send_sem=send_sem.at[step],
                recv_sem=recv_sem.at[me],
                device_id={axis: target},
                device_id_type=MESH,
            )
        )
        arriving.append(
            pltpu.make_async_remote_copy(
                src_ref=source(target),
                dst_ref=place(origin),
                send_sem=send_sem.at[step],
                recv_sem=recv_sem.at[origin],
                device_id={axis: target},
                device_id_type=MESH,
            )
        )
    return out, arriving


def signal_peers():
    barrier = pltpu.get_barrier_semaphore()
    for axis in ("wide", "narrow"):
        size = lax.axis_size(axis)
        me = lax.axis_index(axis)
        for step in range(1, size):
            pl.semaphore_signal(
                barrier, inc=1, device_id={axis: lax.rem(me + step, size)}, device_id_type=MESH
            )


def step_kernel(
    slots_hbm, gcm_hbm, down_hbm, up_hbm, courant_hbm, cloud_hbm, crm_hbm,
    tendency_ref, out_ref,
    slots_ref, gcm_ref, down_ref, up_ref, courant_ref, cloud_ref, crm_ref,
    low_out, high_out, low_in, high_in,
    pick, place, packed, landed, packed_back, landed_back, ranks,
    slab, state, left_gain, middle_gain, keep, push, source_term,
    start_sum, start_sums, moist_sum, moist_sums,
    local_sem, send_sem, recv_sem, back_send, back_recv,
    halo_send, halo_recv, start_send, start_recv, moist_send, moist_recv,
):
    wide = lax.axis_size("wide")
    narrow = lax.axis_size("narrow")
    me = lax.axis_index("wide")
    depth = lax.axis_index("narrow")
    columns = gcm_ref.shape[1]
    rows = packed.shape[0] // wide
    levels, cells = crm_ref.shape[1], crm_ref.shape[2]
    parts = (cells + 2 * SUB) // 8
    bf16 = jnp.bfloat16

    pairs = (
        (crm_hbm.at[1], crm_ref.at[1]),
        (slots_hbm, slots_ref),
        (gcm_hbm, gcm_ref),
        (crm_hbm.at[0], crm_ref.at[0]),
        (courant_hbm, courant_ref),
        (cloud_hbm, cloud_ref),
        (down_hbm, down_ref),
        (up_hbm, up_ref),
    )
    inward = [
        pltpu.make_async_copy(source, dest, local_sem.at[index])
        for index, (source, dest) in enumerate(pairs)
    ]
    crm_moist, slots_copy, gcm_copy, crm_warm, courant_copy, cloud_copy, down_copy, up_copy = inward
    for copy in inward:
        copy.start()
    signal_peers()

    first_half = lax.broadcasted_iota(jnp.int32, (8, columns), 0) < 4

    def pack_halo(field):
        def gather(group, carry):
            low_parts, high_parts = [], []
            for pair in range(2):
                level = group * 4 + pair * 2
                a = crm_ref[field, level, 0:16, :].astype(jnp.float32)[0:8]
                b = crm_ref[field, level + 1, 0:16, :].astype(jnp.float32)[0:8]
                low_parts.append(jnp.where(first_half, a, pltpu.roll(b, 4, 0)))
                a = crm_ref[field, level, cells - 16 : cells, :].astype(jnp.float32)[8:16]
                b = crm_ref[field, level + 1, cells - 16 : cells, :].astype(jnp.float32)[8:16]
                high_parts.append(jnp.where(first_half, pltpu.roll(a, 4, 0), b))
            at = pl.ds(pl.multiple_of(group * 16, 16), 16)
            low_out[field, at, :] = jnp.concatenate(low_parts, axis=0).astype(bf16)
            high_out[field, at, :] = jnp.concatenate(high_parts, axis=0).astype(bf16)
            return carry

        lax.fori_loop(0, levels // 4, gather, 0)

    def halo_copies(field):
        def halo(source, dest, which, step):
            return pltpu.make_async_remote_copy(
                src_ref=source.at[field],
                dst_ref=dest.at[field],
                send_sem=halo_send.at[which],
                recv_sem=halo_recv.at[which],
                device_id={"narrow": lax.rem(depth + step, narrow)},
                device_id_type=MESH,
            )

        return (
            halo(high_out, low_in, 2 * field, 1),
            halo(low_out, high_in, 2 * field + 1, narrow - 1),
        )

    crm_moist.wait()
    pack_halo(1)
    pl.semaphore_wait(pltpu.get_barrier_semaphore(), wide + narrow - 2)
    moist_halo = halo_copies(1)
    for copy in moist_halo:
        copy.start()

    slots_copy.wait()
    mine = slots_ref[pl.ds(me, 1), :]
    owner_first = lax.broadcasted_iota(jnp.int32, (wide, columns), 0) * columns
    goes = (mine >= owner_first) & (mine < owner_first + columns)
    before = (
        lax.broadcasted_iota(jnp.int32, (columns, columns), 0)
        < lax.broadcasted_iota(jnp.int32, (columns, columns), 1)
    ).astype(jnp.float32).astype(bf16)

    def ranked(member):
        member = member.astype(jnp.float32)
        order = jnp.dot(member.astype(bf16), before, preferred_element_type=jnp.float32)
        return jnp.where(member > 0.0, order, -1.0)

    within = lax.broadcasted_iota(jnp.int32, (rows, columns), 0).astype(jnp.float32)
    ranks[...] = ranked(goes)
    for target in range(wide):
        hit = (ranks[target : target + 1, :] == within).astype(jnp.float32).astype(bf16)
        pick[target * rows : (target + 1) * rows, :] = hit
    gcm_copy.wait()
    packed[...] = lax.dot_general(
        pick[...],
        gcm_ref[...].astype(bf16),
        (((1,), (1,)), ((), ())),
        preferred_element_type=jnp.float32,
    ).astype(bf16)
    states, states_in = peers(
        "wide",
        lambda target: on_rows(packed, target * rows, rows),
        lambda origin: on_rows(landed, origin * rows, rows),
        send_sem,
        recv_sem,
    )
    for copy in states:
        copy.start()
    own_rows = pl.ds(pl.multiple_of(me * rows, rows), rows)
    landed[own_rows, :] = packed[own_rows, :]

    crm_warm.wait()
    pack_halo(0)
    warm_halo = halo_copies(0)
    for copy in warm_halo:
        copy.start()

    def spread(level, carry):
        warm = crm_ref[0, level].astype(jnp.float32)
        moist = crm_ref[1, level].astype(jnp.float32)
        slab[level, 8 : cells + 8, :] = warm
        slab[levels + level, 8 : cells + 8, :] = moist
        start_sum[pl.ds(level, 1), :] = jnp.sum(warm + 2.0 * moist, axis=0, keepdims=True)
        return carry

    lax.fori_loop(0, levels, spread, 0, unroll=2)
    starts, starts_in = peers(
        "narrow", lambda target: start_sum, lambda origin: start_sums.at[origin],
        start_send, start_recv,
    )
    for copy in starts:
        copy.start()
    start_sums[depth] = start_sum[...]

    courant_copy.wait()
    cloud_copy.wait()
    courant = courant_ref[...]
    left_gain[...] = (courant + 0.15) * (1.0 / 0.15)
    middle_gain[...] = (0.7 - courant) * (1.0 / 0.15)
    keep[...] = 1.0 - 0.3 * cloud_ref[...].astype(jnp.float32)

    first = me * columns
    slots = slots_ref[...]
    ranks[...] = ranked((slots >= first) & (slots < first + columns))
    slot_number = lax.broadcasted_iota(jnp.int32, (columns, columns), 0) + first
    for origin in range(wide):
        hit = (ranks[origin : origin + 1, :] == within).astype(jnp.float32).astype(bf16)
        spot = (slots_ref[origin : origin + 1, :] == slot_number).astype(jnp.float32)
        place[origin * rows : (origin + 1) * rows, :] = lax.dot_general(
            hit,
            spot.astype(bf16),
            (((1,), (1,)), ((), ())),
            preferred_element_type=jnp.float32,
        ).astype(bf16)
    down_copy.wait()
    for copy in states_in:
        copy.wait_recv()
    by_slot = lax.dot_general(
        landed[...], place[...], (((0,), (0,)), ((), ())), preferred_element_type=jnp.float32
    )
    span = by_slot.shape[0] // 2
    warm_force, moist_force = [
        jnp.dot(
            down_ref[...],
            by_slot[field * span : (field + 1) * span],
            precision=EXACT,
            preferred_element_type=jnp.float32,
        )
        for field in range(2)
    ]
    sum_force = warm_force + 2.0 * moist_force
    source_term[...] = (0.25 * cells * narrow) * sum_force
    for substep in range(SUB):
        gain = 0.25 / SCALE ** (substep + 1)
        push[2 * substep + 1] = gain * moist_force
        push[2 * substep] = gain * sum_force

    def surround(field):
        def insert(group, carry):
            at = pl.ds(pl.multiple_of(group * 16, 16), 16)
            low = low_in[field, at, :].astype(jnp.float32)
            high = high_in[field, at, :].astype(jnp.float32)
            for step in range(4):
                level = group * 4 + step
                from_row = 8 * (step // 2)
                low_part = low[from_row : from_row + 8]
                high_part = high[from_row : from_row + 8]
                if step % 2 == 0:
                    low_part = pltpu.roll(low_part, 4, 0)
                else:
                    high_part = pltpu.roll(high_part, 4, 0)
                slab[field * levels + level, 0:8, :] = low_part
                slab[field * levels + level, cells + 8 : cells + 16, :] = high_part
            return carry

        lax.fori_loop(0, levels // 4, insert, 0)

    def strided(field, level, part):
        return slab[field * levels + level, pl.ds(4 + part, 8, stride=parts), :]

    def advance(field, substep):
        last = substep == SUB - 1

        def fetch(level):
            if substep > 0:
                return [state[field * levels + level, part] for part in range(parts)]
            cell = [strided(field, level, part) for part in range(parts)]
            if field == 1:
                return cell
            return [cell[part] + 2.0 * keep_moist(level, part) for part in range(parts)]

        def across(level):
            cell = fetch(level)
            gain_left = left_gain[pl.ds(level, 1), :]
            gain_middle = middle_gain[pl.ds(level, 1), :]
            behind = [pltpu.roll(cell[-1], 1, 0)] + cell[:-1]
            ahead = cell[1:] + [pltpu.roll(cell[0], 7, 0)]
            return [
                ahead[part] + gain_left * behind[part] + gain_middle * cell[part]
                for part in range(parts)
            ]

        def finish(level, below, here, above):
            forced = push[2 * substep + field, pl.ds(level, 1), :]
            kept = keep[pl.ds(level, 1), :]
            for part in range(parts):
                value = (below[part] + above[part]) + (8.0 * here[part] + forced)
                if field == 1:
                    value = jnp.minimum(value, kept * value)
                if not last:
                    state[field * levels + level, part] = value
                    continue
                value = value * (SCALE**SUB)
                if field == 1:
                    state[levels + level, part] = value
                    slab[2 * levels + level, pl.ds(4 + part, 8, stride=parts), :] = value
                else:
                    value = value - 2.0 * state[levels + level, part]
                    slab[level, pl.ds(4 + part, 8, stride=parts), :] = value

        def climb(level, carry):
            below, here = carry
            above = across(level + 1)
            finish(level, below, here, above)
            return here, above

        bottom = across(0)
        second = across(1)
        finish(0, bottom, bottom, second)
        below, here = lax.fori_loop(1, levels - 1, climb, (bottom, second), unroll=2)
        finish(levels - 1, below, here, here)

    def keep_moist(level, part):
        return strided(1, level, part)

    for copy in moist_halo:
        copy.wait_recv()
    surround(1)
    for substep in range(SUB):
        advance(1, substep)

    def close_moist(level, carry):
        final = slab[2 * levels + level, 8 : cells + 8, :]
        out_ref[1, level] = final.astype(bf16)
        moved = final - slab[levels + level, 8 : cells + 8, :]
        moist_sum[pl.ds(level, 1), :] = jnp.sum(moved, axis=0, keepdims=True)
        return carry

    lax.fori_loop(0, levels, close_moist, 0, unroll=2)
    moists, moists_in = peers(
        "narrow", lambda target: moist_sum, lambda origin: moist_sums.at[origin],
        moist_send, moist_recv,
    )
    for copy in moists:
        copy.start()
    moist_sums[depth] = moist_sum[...]

    for copy in warm_halo:
        copy.wait_recv()
    surround(0)
    for substep in range(SUB - 1):
        advance(0, substep)

    for copy in starts_in + moists_in:
        copy.wait_recv()
    total, moist_change = start_sums[0], moist_sums[0]
    for origin in range(1, narrow):
        total = total + start_sums[origin]
        moist_change = moist_change + moist_sums[origin]
    sum_change = jnp.zeros_like(total)
    for substep in range(SUB):
        over = jnp.concatenate([total[1:], total[-1:]], axis=0)
        under = jnp.concatenate([total[:1], total[:-1]], axis=0)
        rise = 0.1 * (over - 2.0 * total + under) + source_term[...]
        total = total + rise
        sum_change = sum_change + rise
    up_copy.wait()
    changes = (sum_change - 2.0 * moist_change, moist_change)
    tendency = jnp.concatenate(
        [
            lax.dot_general(
                up_ref[...],
                change,
                (((0,), (0,)), ((), ())),
                precision=EXACT,
                preferred_element_type=jnp.float32,
            )
            for change in changes
        ],
        axis=0,
    )
    tendency = (tendency * (1.0 / (cells * narrow * SUB))).astype(bf16)
    packed_back[...] = lax.dot_general(
        place[...], tendency, (((1,), (1,)), ((), ())), preferred_element_type=jnp.float32
    ).astype(bf16)
    back, back_in = peers(
        "wide",
        lambda target: on_rows(packed_back, target * rows, rows),
        lambda origin: on_rows(landed_back, origin * rows, rows),
        back_send,
        back_recv,
    )
    for copy in back:
        copy.start()
    landed_back[own_rows, :] = packed_back[own_rows, :]

    advance(0, SUB - 1)

    def close_warm(level, carry):
        out_ref[0, level] = slab[level, 8 : cells + 8, :].astype(bf16)
        return carry

    lax.fori_loop(0, levels, close_warm, 0, unroll=2)
    for copy in back_in:
        copy.wait_recv()
    tendency_ref[...] = lax.dot_general(
        landed_back[...], pick[...], (((0,), (0,)), ((), ())), preferred_element_type=jnp.float32
    ).astype(bf16)
    for copy in [*moist_halo, *states, *warm_halo, *starts, *moists, *back]:
        copy.wait_send()


def shards(gcm_state, crm_state, courant, cloud_mask, level_down, level_up, column_map):
    wide = lax.axis_size("wide")
    narrow = lax.axis_size("narrow")
    columns, width = gcm_state.shape
    _, levels, cells, _ = crm_state.shape
    capacity = -(-2 * columns // wide)
    rows = -(-capacity // 16) * 16
    total = wide * rows
    operands = (
        column_map.reshape(wide, columns),
        gcm_state.T,
        level_down,
        level_up.T,
        courant,
        cloud_mask,
        crm_state,
    )
    vmem = pl.BlockSpec(memory_space=pltpu.VMEM)
    hbm = pl.BlockSpec(memory_space=pltpu.HBM)
    dma = pltpu.SemaphoreType.DMA
    parts = (cells + 2 * SUB) // 8

    def held(*shape, dtype=jnp.float32):
        return pltpu.VMEM(shape, dtype)

    halo = held(2, levels * SUB, columns, dtype=jnp.bfloat16)
    routed = held(total, columns, dtype=jnp.bfloat16)
    message = held(total, width, dtype=jnp.bfloat16)
    tendency, crm_new = pl.pallas_call(
        step_kernel,
        out_shape=(
            jax.ShapeDtypeStruct((width, columns), jnp.bfloat16),
            jax.ShapeDtypeStruct(crm_state.shape, jnp.bfloat16),
        ),
        in_specs=[hbm] * len(operands),
        out_specs=(vmem, vmem),
        scratch_shapes=[
            *(held(*operand.shape, dtype=operand.dtype) for operand in operands),
            *[halo] * 4,
            *[routed] * 2,
            *[message] * 4,
            held(wide, columns),
            held(3 * levels, cells + 16, columns),
            held(2 * levels, parts, 8, columns),
            *[held(levels, columns)] * 3,
            held(2 * SUB, levels, columns),
            held(levels, columns),
            held(levels, columns),
            held(narrow, levels, columns),
            held(levels, columns),
            held(narrow, levels, columns),
            dma((len(operands) + 1,)),
            *[dma((wide,))] * 4,
            *[dma((4,))] * 2,
            *[dma((narrow,))] * 4,
        ],
        compiler_params=pltpu.CompilerParams(
            collective_id=0, has_side_effects=True, vmem_limit_bytes=40 * 2**20
        ),
        name="step",
    )(*operands)
    return tendency.T, crm_new


def solution(mesh):
    placed = (
        P("wide", None),
        P(None, None, "narrow", "wide"),
        P(None, "wide"),
        P(None, "wide"),
        P(),
        P(),
        P(),
    )
    return jax.shard_map(
        shards,
        mesh=mesh,
        in_specs=placed,
        out_specs=(P("wide", None), P(None, None, "narrow", "wide")),
        check_vma=False,
    )
```

time: 85.6 us -> 35.4 us (0.41)
  other arithmetic: 35.4 us -> 0 us
  Pallas kernels: 0 us -> 26.2 us
  blocking collectives: 20 us -> 0 us
  starting transfers between devices: 12.8 us -> 0 us
  local copies, waits for them, and re-layouts: 11.4 us -> 8.03 us
  waiting for transfers between devices: 3.07 us -> 0 us
  matrix products: 1.19 us -> 0 us
    pallas_call x0 -> x1, Pallas kernels: none -> 26.2 us  [shards(): pl.pallas_call(step_kernel, out_shape=(jax.ShapeDtypeStruct((width, colum...]
    add x12 -> x0, other arithmetic: 23.6 us -> none  [the longest x4 14 us: column_physics(): fields = fields + 0.25 * forcing[:, :, None, :]]
    psum x1 -> x0, blocking collectives: 20 us -> none  [shards(): totals = lax.psum(partial_term, 'narrow').astype(jnp.bfloat16)]
    all_to_all x2 -> x0, starting transfers between devices: 8.97 us -> none  [the longest x1 5.17 us: shards(): lax.all_to_all(packed, 'wide', split_axis=0, concat_axis=0, tiled=True)]
    unnamed x11 -> x16, local copies, waits for them, and re-layouts: 2.04 us -> 8.03 us
    convert_element_type x4 -> x0, other arithmetic: 5.79 us -> none  [the longest x1 3.14 us: shards(): crm_new = fields.astype(jnp.bfloat16)]
    gather x5 -> x0, local copies, waits for them, and re-layouts: 4.74 us -> none  [the longest x1 1.79 us: shards(): totals[slot_of_buffer]]
    slice x9 -> x0, local copies, waits for them, and re-layouts: 4.12 us -> none  [the longest x8 2.95 us: column_physics(): below_cells = jnp.concatenate([fields[:, :1], fields[:, :-1]], axis=1)]
  transfers between devices with their start and end apart: 4 -> 0, of which waited for: 2 -> 0; matrix products, arithmetic and copies ran while one was open for 11% -> 0% of each run, Pallas kernels for 0% -> 0%
where the time goes in v2:
time: 35.4 us; the launch traced here: 34.9 us
  Pallas kernels  26.2 us (74%)
  local copies, waits for them, and re-layouts  8.03 us (23%)
  between operations  0.66 us (2%)
    pallas_call x1, Pallas kernels, shards(): pl.pallas_call(step_kernel, out_shape=(jax.ShapeDtypeStruct((width, colum...  26.2 us
    unnamed x16, local copies, waits for them, and re-layouts  8.03 us

profile of v2, /device:TPU:0, one launch (start us, length us, event | category | flops | bytes accessed | tf_op | source)
XLA Modules:
  0.0 34.9 jit_solution(4024772677390880323)
XLA Ops:
  0.6 0.0 copy-start
  0.6 1.5 %copy-done = bf16[2,60,64,128]{3,2,1,0:T(8,128)(2,1)S(1)} copy-done((bf16[2,60,64,128]{3,2,1,0:T(8,128)(2,1)S(1)}, bf16[2,60,64,128]{3,2,1,0:T(8,128)(2,1)}, u32[]{:S(2)}) %copy-start) | copy-done | bytes 1966104
  2.2 0.0 copy-start.1
  2.2 0.9 %copy-done.1 = f32[128,144]{0,1:T(8,128)S(1)} copy-done((f32[128,144]{0,1:T(8,128)S(1)}, f32[128,144]{0,1:T(8,128)}, u32[]{:S(2)}) %copy-start.1) | copy-done | bytes 73752
  3.1 0.0 copy-start.2
  3.1 0.8 %copy-done.2 = f32[60,72]{1,0:T(8,128)S(1)} copy-done((f32[60,72]{1,0:T(8,128)S(1)}, f32[60,72]{1,0:T(8,128)}, u32[]{:S(2)}) %copy-start.2) | copy-done | bytes 17304
  3.8 0.0 copy-start.3
  3.8 0.8 %copy-done.3 = f32[72,60]{0,1:T(8,128)S(1)} copy-done((f32[72,60]{0,1:T(8,128)S(1)}, f32[72,60]{0,1:T(8,128)}, u32[]{:S(2)}) %copy-start.3) | copy-done | bytes 17304
  4.6 0.0 copy-start.4
  4.6 0.8 %copy-done.4 = f32[60,128]{1,0:T(8,128)S(1)} copy-done((f32[60,128]{1,0:T(8,128)S(1)}, f32[60,128]{1,0:T(8,128)}, u32[]{:S(2)}) %copy-start.4) | copy-done | bytes 30744
  5.3 0.0 copy-start.5
  5.3 0.8 %copy-done.5 = s32[60,128]{1,0:T(8,128)S(1)} copy-done((s32[60,128]{1,0:T(8,128)S(1)}, s32[60,128]{1,0:T(8,128)}, u32[]{:S(2)}) %copy-start.5) | copy-done | bytes 30744
  6.1 0.0 copy-start.6
  6.1 0.7 %copy-done.6 = s32[1024]{0:T(1024)S(1)} copy-done((s32[1024]{0:T(1024)S(1)}, s32[1024]{0:T(1024)}, u32[]{:S(2)}) %copy-start.6) | copy-done | bytes 4120
  6.8 26.2 %step.1 = (bf16[144,128]{1,0:T(8,128)(2,1)S(1)}, bf16[2,60,64,128]{3,2,1,0:T(8,128)(2,1)S(1)}) custom-call(s32[8,128]{1,0:T(8,128)S(1)} %bitcast.7, f32[144,128]{1,0:T(8,128)S(1)} %bitcast.4, f32[60,72]{1,0:T(8,128)S(1)} %copy-done.2, f32[60,72]{1,0:T(8,128)S(1)} %bitcast.6, f32[60,128]{1,0:T(8,128)S(1)} %copy-done.4, s32[60,128]{1,0:T(8,128)S(1)} %copy-done.5, ...), custom_call_target="tpu_custom_call" | custom-call | tf_op jit(solution)/shard_map/step/pallas_call | solution.py:439
  33.0 0.6 %copy.11 = bf16[128,144]{0,1:T(8,128)(2,1)} copy(bf16[128,144]{0,1:T(8,128)(2,1)S(1)} %bitcast.5) | data formatting | bytes 73728
  33.6 1.3 %copy.12 = bf16[2,60,64,128]{3,2,1,0:T(8,128)(2,1)} copy(bf16[2,60,64,128]{3,2,1,0:T(8,128)(2,1)S(1)} %get-tuple-element.9) | data formatting | bytes 3932160
Async XLA Ops:
  0.6 1.5 %copy-start = (bf16[2,60,64,128]{3,2,1,0:T(8,128)(2,1)S(1)}, bf16[2,60,64,128]{3,2,1,0:T(8,128)(2,1)}, u32[]{:S(2)}) copy-start(bf16[2,60,64,128]{3,2,1,0:T(8,128)(2,1)} %crm_hbm.1) | copy-start | bytes 5898244
  2.2 0.9 %copy-start.1 = (f32[128,144]{0,1:T(8,128)S(1)}, f32[128,144]{0,1:T(8,128)}, u32[]{:S(2)}) copy-start(f32[128,144]{0,1:T(8,128)} %param.7) | copy-start | bytes 221188
  3.1 0.8 %copy-start.2 = (f32[60,72]{1,0:T(8,128)S(1)}, f32[60,72]{1,0:T(8,128)}, u32[]{:S(2)}) copy-start(f32[60,72]{1,0:T(8,128)} %down_hbm.1) | copy-start | bytes 51844
  3.8 0.8 %copy-start.3 = (f32[72,60]{0,1:T(8,128)S(1)}, f32[72,60]{0,1:T(8,128)}, u32[]{:S(2)}) copy-start(f32[72,60]{0,1:T(8,128)} %param.12) | copy-start | bytes 51844
  4.6 0.8 %copy-start.4 = (f32[60,128]{1,0:T(8,128)S(1)}, f32[60,128]{1,0:T(8,128)}, u32[]{:S(2)}) copy-start(f32[60,128]{1,0:T(8,128)} %courant_hbm.1) | copy-start | bytes 92164
  5.3 0.8 %copy-start.5 = (s32[60,128]{1,0:T(8,128)S(1)}, s32[60,128]{1,0:T(8,128)}, u32[]{:S(2)}) copy-start(s32[60,128]{1,0:T(8,128)} %cloud_hbm.1) | copy-start | bytes 92164
  6.1 0.7 %copy-start.6 = (s32[1024]{0:T(1024)S(1)}, s32[1024]{0:T(1024)}, u32[]{:S(2)}) copy-start(s32[1024]{0:T(1024)} %param.13) | copy-start | bytes 12292

commit v3 on v2

--- a/solution.py
+++ b/solution.py
@@ -58,8 +58,8 @@
 
 def step_kernel(
     slots_hbm, gcm_hbm, down_hbm, up_hbm, courant_hbm, cloud_hbm, crm_hbm,
-    tendency_ref, out_ref,
-    slots_ref, gcm_ref, down_ref, up_ref, courant_ref, cloud_ref, crm_ref,
+    tendency_ref, out_hbm,
+    out_ref, slots_ref, gcm_ref, down_ref, up_ref, courant_ref, cloud_ref, crm_ref,
     low_out, high_out, low_in, high_in,
     pick, place, packed, landed, packed_back, landed_back, ranks,
     slab, state, left_gain, middle_gain, keep, push, source_term,
@@ -335,6 +335,9 @@
         return carry
 
     lax.fori_loop(0, levels, close_moist, 0, unroll=2)
+    moist_out = pltpu.make_async_copy(out_ref.at[1], out_hbm.at[1], local_sem.at[len(pairs)])
+    warm_out = pltpu.make_async_copy(out_ref.at[0], out_hbm.at[0], local_sem.at[len(pairs) + 1])
+    moist_out.start()
     moists, moists_in = peers(
         "narrow", lambda target: moist_sum, lambda origin: moist_sums.at[origin],
         moist_send, moist_recv,
@@ -399,6 +402,7 @@
         return carry
 
     lax.fori_loop(0, levels, close_warm, 0, unroll=2)
+    warm_out.start()
     for copy in back_in:
         copy.wait_recv()
     tendency_ref[...] = lax.dot_general(
@@ -406,6 +410,8 @@
     ).astype(bf16)
     for copy in [*moist_halo, *states, *warm_halo, *starts, *moists, *back]:
         copy.wait_send()
+    moist_out.wait()
+    warm_out.wait()
 
 
 def shards(gcm_state, crm_state, courant, cloud_mask, level_down, level_up, column_map):
@@ -443,8 +449,9 @@
             jax.ShapeDtypeStruct(crm_state.shape, jnp.bfloat16),
         ),
         in_specs=[hbm] * len(operands),
-        out_specs=(vmem, vmem),
+        out_specs=(vmem, hbm),
         scratch_shapes=[
+            held(*crm_state.shape, dtype=jnp.bfloat16),
             *(held(*operand.shape, dtype=operand.dtype) for operand in operands),
             *[halo] * 4,
             *[routed] * 2,
@@ -459,13 +466,13 @@
             held(narrow, levels, columns),
             held(levels, columns),
             held(narrow, levels, columns),
-            dma((len(operands) + 1,)),
+            dma((len(operands) + 3,)),
             *[dma((wide,))] * 4,
             *[dma((4,))] * 2,
             *[dma((narrow,))] * 4,
         ],
         compiler_params=pltpu.CompilerParams(
-            collective_id=0, has_side_effects=True, vmem_limit_bytes=40 * 2**20
+            collective_id=0, has_side_effects=True, vmem_limit_bytes=60 * 2**20
         ),
         name="step",
     )(*operands)

time: 35.4 us -> 31.3 us (0.88)
  local copies, waits for them, and re-layouts: 8.03 us -> 4.36 us
    unnamed x16 -> x2, local copies, waits for them, and re-layouts: 8.03 us -> 4.36 us
where the time goes in v3:
time: 31.3 us; the launch traced here: 31 us
  Pallas kernels  26 us (83%)
  local copies, waits for them, and re-layouts  4.36 us (14%)
  between operations  0.64 us (2%)
    pallas_call x1, Pallas kernels, shards(): pl.pallas_call(step_kernel, out_shape=(jax.ShapeDtypeStruct((width, colum...  26 us
    unnamed x2, local copies, waits for them, and re-layouts  4.36 us

profile of v3, /device:TPU:0, one launch (start us, length us, event | category | flops | bytes accessed | tf_op | source)
XLA Modules:
  0.0 31.0 jit_solution(14410267786299239380)
XLA Ops:
  0.6 26.0 %step.1 = (bf16[144,128]{1,0:T(8,128)(2,1)}, bf16[2,60,64,128]{3,2,1,0:T(8,128)(2,1)}) custom-call(s32[8,128]{1,0:T(8,128)} %bitcast.7, f32[144,128]{1,0:T(8,128)} %bitcast.4, f32[60,72]{1,0:T(8,128)} %down_hbm.1, f32[60,72]{1,0:T(8,128)} %bitcast.6, f32[60,128]{1,0:T(8,128)} %courant_hbm.1, s32[60,128]{1,0:T(8,128)} %cloud_hbm.1, ...), custom_call_target="tpu_custom_call" | custom-call | tf_op jit(solution)/shard_map/step/pallas_call | solution.py:445
  26.7 1.4 %copy.11 = bf16[128,144]{0,1:T(8,128)(2,1)} copy(bf16[128,144]{0,1:T(8,128)(2,1)} %bitcast.5) | data formatting | bytes 73728
  28.1 3.0 %copy.12 = bf16[2,60,64,128]{3,2,1,0:T(8,128)(2,1)} copy(bf16[2,60,64,128]{3,2,1,0:T(8,128)(2,1)} %get-tuple-element.9) | data formatting | bytes 3932160
